TPU v7x, 256 devices: a whole 4x4x8 slice. The times are simulated.
256 devices in a mesh: dp: 32 (over x_hi, z, core), mp: 8 (over y, x_lo).
Axes of the slice: x: 4 (x_hi: 2, x_lo: 2; x = x_hi * 2 + x_lo), y: 4, z: 8, core: 2. Of those that a mesh axis runs over, the one named last changes fastest.
Arguments:
- acts: bfloat16 [32768, 8192], P('dp', 'mp'), may hold values from -6 to 6
- cotangent: bfloat16 [32768, 8, 256], P('dp', 'mp'), may hold values from -0.03125 to 0.03125
- master: float32 [8192, 8, 256], P('dp', 'mp'), may hold values from -0.0625 to 0.0625
- first_moment: float32 [8192, 8, 256], P('dp', 'mp'), may hold values from -6 to 6
- second_moment: float32 [8192, 8, 256], P('dp', 'mp'), may hold values from 0.25 to 4
- long_acts: bfloat16 [8192, 8192], P('dp'), may hold values from -6 to 6
Outputs:
- new_master: float32 [8192, 8, 256], P(('dp', 'mp'))
- new_first: float32 [8192, 8, 256], P(('dp', 'mp'))
- new_second: float32 [8192, 8, 256], P(('dp', 'mp'))
- long_kv: bfloat16 [8192, 8, 256], P('dp', 'mp')
All inputs are finite; a program needn't handle non-finite values.
Results may differ from a plain program's by a relative error of at most 0.005.
Values may be sent and summed in bfloat16 or wider, within the bound.
A program may use at most 128 MiB of HBM per device.

v0:
```python
import jax
import jax.numpy as jnp
from jax import lax
from jax.sharding import PartitionSpec as P

beta_one = 0.9
beta_two = 0.95
learn_rate = 0.001
decay_rate = 0.1
adam_eps = 1e-08
steps_done = 100


def on_device(acts, cotangent, master, first_moment, second_moment, long_acts):
    gathered = lax.all_gather(acts, "mp", axis=1, tiled=True)
    flat_cot = cotangent.reshape(cotangent.shape[0], -1)
    columns = gathered
    product = lax.dot_general(
        columns, flat_cot, (((0,), (0,)), ((), ())), preferred_element_type=jnp.float32
    )
    grad = lax.psum_scatter(
        product.reshape(
            lax.axis_size("dp") * master.shape[0], master.shape[1], master.shape[2]
        ).astype(jnp.bfloat16),
        "dp",
        scatter_dimension=0,
        tiled=True,
    ).astype(jnp.float32)
    first_next = beta_one * first_moment + (1.0 - beta_one) * grad
    second_next = beta_two * second_moment + (1.0 - beta_two) * grad * grad
    fix_one = 1.0 - beta_one**steps_done
    fix_two = 1.0 - beta_two**steps_done
    update = (
        first_next / fix_one / (jnp.sqrt(second_next / fix_two) + adam_eps) + decay_rate * master
    )
    master_next = master - learn_rate * update
    new_master, new_first, new_second = (
        lax.all_to_all(master_next, "mp", split_axis=0, concat_axis=1, tiled=True),
        lax.all_to_all(first_next, "mp", split_axis=0, concat_axis=1, tiled=True),
        lax.all_to_all(second_next, "mp", split_axis=0, concat_axis=1, tiled=True),
    )
    weights = new_master.astype(jnp.bfloat16)
    long_rows = long_acts.shape[0]
    split_acts = long_acts.reshape(long_rows, lax.axis_size("dp"), lax.axis_size("mp"), -1)
    stripe = lax.dynamic_index_in_dim(split_acts, lax.axis_index("mp"), 2, keepdims=False).reshape(
        long_rows, -1
    )
    piece = lax.all_gather(weights, "dp", axis=0, tiled=True)
    columns = stripe
    partial_kv = jnp.dot(
        columns, piece.reshape(piece.shape[0], -1), preferred_element_type=jnp.float32
    )
    partial_kv = partial_kv.reshape(long_rows, weights.shape[1], weights.shape[2])
    long_kv = lax.psum_scatter(partial_kv, "mp", scatter_dimension=1, tiled=True).astype(
        jnp.bfloat16
    )
    return (new_master, new_first, new_second, long_kv)


def solution(mesh):
    in_specs = (
        P("dp", "mp"),
        P("dp", "mp", None),
        P("dp", "mp", None),
        P("dp", "mp", None),
        P("dp", "mp", None),
        P("dp", None),
    )
    out_specs = (
        P(("dp", "mp"), None, None),
        P(("dp", "mp"), None, None),
        P(("dp", "mp"), None, None),
        P("dp", "mp", None),
    )
    return jax.shard_map(
        on_device, mesh=mesh, in_specs=in_specs, out_specs=out_specs, check_vma=False
    )
```

profile of v0, /device:TPU:1, one launch (start us, length us, event | category | flops | bytes accessed | tf_op | source)
XLA Modules:
  0.0 656.2 jit_solution(6705560739923045763)
XLA Ops:
  7.2 0.0 copy-start
  7.2 0.0 all-gather.3.cloned.1.call-start
  7.2 0.7 all-gather.3.cloned.1.call-update
  7.9 0.0 reduce-scatter.3.cloned.1.call-start
  8.0 333.8 %all-gather.3.cloned.1.call-done = bf16[1024,8192]{1,0:T(8,128)(2,1)} async-done(((bf16[1024,1024]{1,0:T(8,128)(2,1)}), bf16[1024,8192]{1,0:T(8,128)(2,1)}) %all-gather.3.cloned.1.call-update) | async-done | bytes 16777232 | tf_op jit(solution)/shard_map/all_gather | solution.py:15
  341.8 12.5 %fusion = bf16[8192,1,256]{2,0,1:T(8,128)(2,1)} fusion(bf16[1024,8192]{1,0:T(8,128)(2,1)} %all-gather.3.cloned.1.call-done, bf16[1024,1,256]{2,0,1:T(8,128)(2,1)S(1)} %copy-done), kind=kOutput, calls=%fused_computation.1 | convolution fusion | flops 4297064448 | bytes 21495808 | tf_op jit(solution)/shard_map/dot_general | solution.py:18
  354.4 0.0 reduce-scatter.3.cloned.1.call-update
  354.4 0.0 all-gather.5.cloned.1.call-start
  354.4 124.1 %reduce-scatter.3.cloned.1.call-done = bf16[256,1,256]{2,0,1:T(8,128)(2,1)} async-done(((bf16[8192,1,256]{2,0,1:T(8,128)(2,1)}), bf16[256,1,256]{2,0,1:T(8,128)(2,1)}) %reduce-scatter.3.cloned.1.call-update) | async-done | bytes 131088 | tf_op jit(solution)/shard_map/reduce_scatter | solution.py:21
  478.5 0.0 copy-done.1
  478.5 1.1 multiply_subtract_fusion
  479.7 0.3 copy.33
  479.9 10.3 %all_to_all.54 = f32[256,1,256]{2,1,0:T(1,128)S(1)} all-to-all(f32[256,1,256]{2,1,0:T(1,128)S(1)} %copy.33), channel_id=1, replica_groups=mesh['dp'=32,'mp'=8] {'mp'}, dimensions={0} | all-to-all | bytes 524288 | tf_op jit(solution)/shard_map/all_to_all | solution.py:38
  490.2 0.9 fusion.6
  491.1 0.0 all-gather.5.cloned.1.call-update
  491.2 0.0 reduce-scatter.5.cloned.1.call-start
  491.2 6.5 copy.39
  497.7 1.1 constant_dynamic-slice_fusion
  498.8 82.5 %all-gather.5.cloned.1.call-done = bf16[1024,8,256]{2,1,0:T(8,128)(2,1)} async-done(((bf16[32,8,256]{2,1,0:T(8,128)(2,1)}), bf16[1024,8,256]{2,1,0:T(8,128)(2,1)}) %all-gather.5.cloned.1.call-update) | async-done | bytes 4194320 | tf_op jit(solution)/shard_map/all_gather | solution.py:48
  581.2 6.7 %copy.44 = bf16[1024,8,256]{0,2,1:T(8,128)(2,1)} copy(bf16[1024,8,256]{2,1,0:T(8,128)(2,1)} %all-gather.5.cloned.1.call-done) | data formatting | bytes 8388608 | tf_op jit(solution)/shard_map/reshape | solution.py:51
  588.0 4.8 fusion.1
  592.8 0.0 reduce-scatter.5.cloned.1.call-update
  592.8 1.0 copy.35
  593.8 4.0 all-to-all-start.1
  597.8 1.0 copy.37
  598.8 5.6 all-to-all-done.1
  604.4 3.4 all-to-all-start.2
  607.8 0.9 copy.59
  608.6 8.6 %all-to-all-done.2 = f32[256,1,256]{2,1,0:T(1,128)S(1)} async-done(((f32[256,1,256]{2,1,0:T(1,128)}), f32[256,1,256]{2,1,0:T(1,128)S(1)}, u32[]{:S(2)}, u32[]{:S(2)}) %all-to-all-start.2) | async-done | bytes 262176 | tf_op jit(solution)/shard_map/all_to_all | solution.py:40
  617.3 0.9 copy.58
  618.1 29.9 %reduce-scatter.5.cloned.1.call-done = f32[256,1,256]{2,0,1:T(8,128)} async-done(((f32[256,8,256]{2,0,1:T(8,128)}), f32[256,1,256]{2,0,1:T(8,128)}) %reduce-scatter.5.cloned.1.call-update) | async-done | bytes 262160 | tf_op jit(solution)/shard_map/reduce_scatter | solution.py:54
  648.0 1.6 convert_element_type.19
  (6 shorter events, 0.0 us)
Async XLA Ops:
  7.2 334.6 %copy-start = (bf16[1024,1,256]{2,0,1:T(8,128)(2,1)S(1)}, bf16[1024,1,256]{2,0,1:T(8,128)(2,1)}, u32[]{:S(2)}) copy-start(bf16[1024,1,256]{2,0,1:T(8,128)(2,1)} %param.7) | copy-start | bytes 1572868
  7.2 334.6 %all-gather.3.cloned.1.call-start = ((), (), s32[]{:S(2)}) async-start(), calls=%async_computation.5 | async-start | bytes 18874368 | tf_op jit(solution)/shard_map/all_gather | solution.py:15
  7.9 470.6 %reduce-scatter.3.cloned.1.call-start = ((), (), s32[]{:S(2)}) async-start(), calls=%async_computation.6 | async-start | bytes 4325376 | tf_op jit(solution)/shard_map/reduce_scatter | solution.py:21
  354.4 124.2 %copy-start.1 = (f32[256,1,256]{2,1,0:T(1,128)S(1)}, f32[256,1,256]{2,1,0:T(1,128)}, u32[]{:S(2)}) copy-start(f32[256,1,256]{2,1,0:T(1,128)} %param.8) | copy-start | bytes 786436
  354.4 124.2 %copy-start.2 = (f32[256,1,256]{2,1,0:T(1,128)S(1)}, f32[256,1,256]{2,1,0:T(1,128)}, u32[]{:S(2)}) copy-start(f32[256,1,256]{2,1,0:T(1,128)} %param.9) | copy-start | bytes 786436
  354.4 124.2 %copy-start.3 = (f32[256,1,256]{2,1,0:T(1,128)S(1)}, f32[256,1,256]{2,1,0:T(1,128)}, u32[]{:S(2)}) copy-start(f32[256,1,256]{2,1,0:T(1,128)} %param.10) | copy-start | bytes 786436
  354.4 226.9 %all-gather.5.cloned.1.call-start = ((), (), s32[]{:S(2)}) async-start(), calls=%async_computation.7 | async-start | bytes 4325376 | tf_op jit(solution)/shard_map/all_gather | solution.py:48
  491.2 156.8 %reduce-scatter.5.cloned.1.call-start = ((), (), s32[]{:S(2)}) async-start(), calls=%async_computation.8 | async-start | bytes 2359296 | tf_op jit(solution)/shard_map/reduce_scatter | solution.py:54
  593.8 10.6 %all-to-all-start.1 = ((f32[256,1,256]{2,1,0:T(1,128)}), f32[256,1,256]{2,1,0:T(1,128)S(1)}, u32[]{:S(2)}, u32[]{:S(2)}) async-start(f32[256,1,256]{2,1,0:T(1,128)} %copy.35), calls=%async_computation.2 | async-start | bytes 524288 | tf_op jit(solution)/shard_map/all_to_all | solution.py:39
  604.4 12.9 %all-to-all-start.2 = ((f32[256,1,256]{2,1,0:T(1,128)}), f32[256,1,256]{2,1,0:T(1,128)S(1)}, u32[]{:S(2)}, u32[]{:S(2)}) async-start(f32[256,1,256]{2,1,0:T(1,128)} %copy.37), calls=%async_computation.3 | async-start | bytes 524288 | tf_op jit(solution)/shard_map/all_to_all | solution.py:40
Sparse Core Ops, SparseCore 0:
  9.8 331.9 all-gather.2
  354.5 123.9 reduce-scatter.2
  491.3 89.9 all-gather.4
  592.9 55.0 reduce-scatter.4
where the time goes:
time: 657 us; the launch traced here: 656 us
  waiting for transfers between devices  585 us (89%)
  local copies, waits for them, and re-layouts  18.2 us (3%)
  matrix products  17.4 us (3%)
  between operations  13.8 us (2%)
  blocking collectives  10.3 us (2%)
  starting transfers between devices  7.59 us (1%)
    all_gather x1, waiting for transfers between devices, on_device(): gathered = lax.all_gather(acts, 'mp', axis=1, tiled=True)  334 us
    reduce_scatter x1, waiting for transfers between devices, on_device(): lax.psum_scatter(product.reshape(lax.axis_size('dp') * master.shape[0], m...  124 us
    all_gather x1, waiting for transfers between devices, on_device(): piece = lax.all_gather(weights, 'dp', axis=0, tiled=True)  82.5 us
    reduce_scatter x1, waiting for transfers between devices, on_device(): lax.psum_scatter(partial_kv, 'mp', scatter_dimension=1, tiled=True)  29.9 us
  transfers between devices with their start and end apart: 6, of which 6 were waited for; matrix products, arithmetic and copies ran while one was open for 2% of the time, Pallas kernels for 0%

commit v1 on v0

--- a/solution.py
+++ b/solution.py
@@ -45,7 +45,9 @@
     stripe = lax.dynamic_index_in_dim(split_acts, lax.axis_index("mp"), 2, keepdims=False).reshape(
         long_rows, -1
     )
-    piece = lax.all_gather(weights, "dp", axis=0, tiled=True)
+    piece = jnp.concatenate(
+        lax.all_to_all(jnp.stack([weights] * lax.axis_size("dp")), "dp", 0, 0), axis=0
+    )
     columns = stripe
     partial_kv = jnp.dot(
         columns, piece.reshape(piece.shape[0], -1), preferred_element_type=jnp.float32

time: 657 us -> 684 us (1.041)
  starting transfers between devices: 7.59 us -> 20.6 us
  local copies, waits for them, and re-layouts: 18.2 us -> 25.9 us
    all_to_all x0 -> x1, waiting for transfers between devices: none -> 88.6 us  [on_device(): lax.all_to_all(jnp.stack([weights] * lax.axis_size('dp')), 'dp', 0, 0)]
    all_gather x1 -> x0, waiting for transfers between devices: 82.5 us -> none  [on_device(): piece = lax.all_gather(weights, 'dp', axis=0, tiled=True)]
    all_to_all x0 -> x1, starting transfers between devices: none -> 13.6 us  [on_device(): lax.all_to_all(jnp.stack([weights] * lax.axis_size('dp')), 'dp', 0, 0)]
where the time goes in v1:
time: 684 us; the launch traced here: 683 us
  waiting for transfers between devices  591 us (86%)
  local copies, waits for them, and re-layouts  25.9 us (4%)
  starting transfers between devices  20.6 us (3%)
  matrix products  17.4 us (3%)
  between operations  13.8 us (2%)
  blocking collectives  10.3 us (2%)
    all_gather x1, waiting for transfers between devices, on_device(): gathered = lax.all_gather(acts, 'mp', axis=1, tiled=True)  334 us
    reduce_scatter x1, waiting for transfers between devices, on_device(): lax.psum_scatter(product.reshape(lax.axis_size('dp') * master.shape[0], m...  124 us
    all_to_all x1, waiting for transfers between devices, on_device(): lax.all_to_all(jnp.stack([weights] * lax.axis_size('dp')), 'dp', 0, 0)  88.6 us
    reduce_scatter x1, waiting for transfers between devices, on_device(): lax.psum_scatter(partial_kv, 'mp', scatter_dimension=1, tiled=True)  29.9 us
  transfers between devices with their start and end apart: 6, of which 6 were waited for; matrix products, arithmetic and copies ran while one was open for 2% of the time, Pallas kernels for 0%

profile of v1, /device:TPU:1, one launch (start us, length us, event | category | flops | bytes accessed | tf_op | source)
XLA Modules:
  0.0 682.9 jit_solution(8146334458015027560)
XLA Ops:
  7.2 0.0 copy-start
  7.2 0.0 all-gather.2.cloned.1.call-start
  7.2 0.7 all-gather.2.cloned.1.call-update
  7.9 0.0 reduce-scatter.3.cloned.1.call-start
  8.0 333.8 %all-gather.2.cloned.1.call-done = bf16[1024,8192]{1,0:T(8,128)(2,1)} async-done(((bf16[1024,1024]{1,0:T(8,128)(2,1)}), bf16[1024,8192]{1,0:T(8,128)(2,1)}) %all-gather.2.cloned.1.call-update) | async-done | bytes 16777232 | tf_op jit(solution)/shard_map/all_gather | solution.py:15
  341.8 12.5 %fusion = bf16[8192,1,256]{2,0,1:T(8,128)(2,1)} fusion(bf16[1024,8192]{1,0:T(8,128)(2,1)} %all-gather.2.cloned.1.call-done, bf16[1024,1,256]{2,0,1:T(8,128)(2,1)S(1)} %copy-done), kind=kOutput, calls=%fused_computation.1 | convolution fusion | flops 4297064448 | bytes 21495808 | tf_op jit(solution)/shard_map/dot_general | solution.py:18
  354.3 0.0 reduce-scatter.3.cloned.1.call-update
  354.4 124.1 %reduce-scatter.3.cloned.1.call-done = bf16[256,1,256]{2,0,1:T(8,128)(2,1)} async-done(((bf16[8192,1,256]{2,0,1:T(8,128)(2,1)}), bf16[256,1,256]{2,0,1:T(8,128)(2,1)}) %reduce-scatter.3.cloned.1.call-update) | async-done | bytes 131088 | tf_op jit(solution)/shard_map/reduce_scatter | solution.py:21
  478.5 1.1 multiply_subtract_fusion
  479.6 0.3 copy.33
  479.9 10.3 %all_to_all.59 = f32[256,1,256]{2,1,0:T(1,128)S(1)} all-to-all(f32[256,1,256]{2,1,0:T(1,128)S(1)} %copy.33), channel_id=1, replica_groups=mesh['dp'=32,'mp'=8] {'mp'}, dimensions={0} | all-to-all | bytes 524288 | tf_op jit(solution)/shard_map/all_to_all | solution.py:38
  490.2 0.9 fusion.4
  491.1 2.4 stack.2
  493.5 13.6 %all-to-all-start.3 = ((bf16[32,32,8,256]{3,2,1,0:T(8,128)(2,1)}), bf16[32,32,8,256]{3,2,1,0:T(8,128)(2,1)}, u32[]{:S(2)}, u32[]{:S(2)}) async-start(bf16[32,32,8,256]{3,2,1,0:T(8,128)(2,1)} %stack.2), calls=%async_computation.4 | async-start | bytes 8388608 | tf_op jit(solution)/shard_map/all_to_all | solution.py:49
  507.1 0.0 reduce-scatter.5.cloned.1.call-start
  507.2 6.4 copy.39
  513.6 1.1 constant_dynamic-slice_fusion
  514.7 88.6 %all-to-all-done.3 = bf16[32,32,8,256]{3,2,1,0:T(8,128)(2,1)} async-done(((bf16[32,32,8,256]{3,2,1,0:T(8,128)(2,1)}), bf16[32,32,8,256]{3,2,1,0:T(8,128)(2,1)}, u32[]{:S(2)}, u32[]{:S(2)}) %all-to-all-start.3) | async-done | bytes 4194336 | tf_op jit(solution)/shard_map/all_to_all | solution.py:49
  603.3 5.6 copy.44
  608.9 6.4 copy.40
  615.4 4.8 fusion.7
  620.2 0.0 reduce-scatter.5.cloned.1.call-update
  620.2 1.0 copy.35
  621.2 3.4 all-to-all-start.1
  624.6 1.0 copy.37
  625.6 5.2 all-to-all-done.1
  630.7 3.4 all-to-all-start.2
  634.1 0.9 copy.59
  635.0 9.0 %all-to-all-done.2 = f32[256,1,256]{2,1,0:T(1,128)S(1)} async-done(((f32[256,1,256]{2,1,0:T(1,128)}), f32[256,1,256]{2,1,0:T(1,128)S(1)}, u32[]{:S(2)}, u32[]{:S(2)}) %all-to-all-start.2) | async-done | bytes 262176 | tf_op jit(solution)/shard_map/all_to_all | solution.py:40
  644.0 0.9 copy.58
  644.8 29.9 %reduce-scatter.5.cloned.1.call-done = f32[256,1,256]{2,0,1:T(8,128)} async-done(((f32[256,8,256]{2,0,1:T(8,128)}), f32[256,1,256]{2,0,1:T(8,128)}) %reduce-scatter.5.cloned.1.call-update) | async-done | bytes 262160 | tf_op jit(solution)/shard_map/reduce_scatter | solution.py:56
  674.8 1.6 convert_element_type.21
  (7 shorter events, 0.0 us)
Async XLA Ops:
  7.2 334.6 %copy-start = (bf16[1024,1,256]{2,0,1:T(8,128)(2,1)S(1)}, bf16[1024,1,256]{2,0,1:T(8,128)(2,1)}, u32[]{:S(2)}) copy-start(bf16[1024,1,256]{2,0,1:T(8,128)(2,1)} %param.7) | copy-start | bytes 1572868
  7.2 334.6 %all-gather.2.cloned.1.call-start = ((), (), s32[]{:S(2)}) async-start(), calls=%async_computation.6 | async-start | bytes 18874368 | tf_op jit(solution)/shard_map/all_gather | solution.py:15
  7.9 470.6 %reduce-scatter.3.cloned.1.call-start = ((), (), s32[]{:S(2)}) async-start(), calls=%async_computation.7 | async-start | bytes 4325376 | tf_op jit(solution)/shard_map/reduce_scatter | solution.py:21
  354.3 124.2 %copy-start.1 = (f32[256,1,256]{2,1,0:T(1,128)S(1)}, f32[256,1,256]{2,1,0:T(1,128)}, u32[]{:S(2)}) copy-start(f32[256,1,256]{2,1,0:T(1,128)} %param.8) | copy-start | bytes 786436
  354.3 124.2 %copy-start.2 = (f32[256,1,256]{2,1,0:T(1,128)S(1)}, f32[256,1,256]{2,1,0:T(1,128)}, u32[]{:S(2)}) copy-start(f32[256,1,256]{2,1,0:T(1,128)} %param.9) | copy-start | bytes 786436
  354.3 124.2 %copy-start.3 = (f32[256,1,256]{2,1,0:T(1,128)S(1)}, f32[256,1,256]{2,1,0:T(1,128)}, u32[]{:S(2)}) copy-start(f32[256,1,256]{2,1,0:T(1,128)} %param.10) | copy-start | bytes 786436
  493.5 109.8 %all-to-all-start.3 = ((bf16[32,32,8,256]{3,2,1,0:T(8,128)(2,1)}), bf16[32,32,8,256]{3,2,1,0:T(8,128)(2,1)}, u32[]{:S(2)}, u32[]{:S(2)}) async-start(bf16[32,32,8,256]{3,2,1,0:T(8,128)(2,1)} %stack.2), calls=%async_computation.4 | async-start | bytes 8388608 | tf_op jit(solution)/shard_map/all_to_all | solution.py:49
  507.1 167.6 %reduce-scatter.5.cloned.1.call-start = ((), (), s32[]{:S(2)}) async-start(), calls=%async_computation.8 | async-start | bytes 2359296 | tf_op jit(solution)/shard_map/reduce_scatter | solution.py:56
  621.2 9.5 %all-to-all-start.1 = ((f32[256,1,256]{2,1,0:T(1,128)}), f32[256,1,256]{2,1,0:T(1,128)S(1)}, u32[]{:S(2)}, u32[]{:S(2)}) async-start(f32[256,1,256]{2,1,0:T(1,128)} %copy.35), calls=%async_computation.2 | async-start | bytes 524288 | tf_op jit(solution)/shard_map/all_to_all | solution.py:39
  630.7 13.3 %all-to-all-start.2 = ((f32[256,1,256]{2,1,0:T(1,128)}), f32[256,1,256]{2,1,0:T(1,128)S(1)}, u32[]{:S(2)}, u32[]{:S(2)}) async-start(f32[256,1,256]{2,1,0:T(1,128)} %copy.37), calls=%async_computation.3 | async-start | bytes 524288 | tf_op jit(solution)/shard_map/all_to_all | solution.py:40
Sparse Core Ops, SparseCore 0:
  9.8 331.9 all-gather.1
  354.5 123.9 reduce-scatter.2
  620.3 54.3 reduce-scatter.4
